TPU v7x, 32 devices: a whole 2x2x4 slice. The times are simulated.
32 devices in a mesh: region: 4 (over z), sub: 8 (over y, x, core).
Axes of the slice: x: 2, y: 2, z: 4, core: 2. Of those that a mesh axis runs over, the one named last changes fastest.
Arguments:
- features: bfloat16 [96, 262144], P(None, ('region', 'sub')), may hold values from -60 to 60
- neighbors: int32 [27, 262144], P(None, ('region', 'sub')), may hold values from 0 to 12288, as said below
- send_rows: int32 [32, 4096], P(('region', 'sub')), may hold values from 0 to 8191, as said below
- active_rows: int32 [32], replicated, may hold values from 2048 to 8192, as said below
- weight_one: bfloat16 [27, 96, 96], replicated, may hold values from -0.125 to 0.125
- weight_two: bfloat16 [27, 96, 96], replicated, may hold values from -0.125 to 0.125
- norm_gain: float32 [2, 96], replicated, may hold values from 0.5 to 2
- norm_shift: float32 [2, 96], replicated, may hold values from -1 to 1
Outputs:
- refined: bfloat16 [96, 262144], P(None, ('region', 'sub'))
Inputs may be any that keep to these rules, and one draw needn't show every extreme that they name: `active_rows`: each entry is a multiple of 128; the busiest device has all 8192 slots occupied; occupied slots come first. `send_rows`: row s lists in slots r * 128 to r * 128 + 127 the local columns of device s, below active_rows[s], whose features device r needs; any device r other than s may receive; the slots that carry voxels come first in each group of 128; a slot that carries nothing holds 0; in every draw some device receives all 128 slots from every other device. `neighbors`: an entry is a local column below the device's active count, an arrived column 8192 + p * 128 + c whose slot carries a voxel, or 12288 for a missing voxel; the middle offset of an active column names the column itself; inactive columns name no voxel; every slot that carries a voxel is named somewhere.
All inputs are finite; a program needn't handle non-finite values.
Results may differ from a plain program's by a relative error of at most 0.0052.
Values may be sent and summed in bfloat16 or wider, within the bound.
A program may use at most 128 MiB of HBM per device.

v0:
```python
import jax
import jax.numpy as jnp
from jax import lax
from jax.sharding import PartitionSpec as P

BLOCK = 128


NORM_EPS = 1e-05


def convolve(extended, kernel_map, weight):
    extent = kernel_map.shape[1]
    channels = extended.shape[0]
    table = jnp.concatenate(
        [jnp.transpose(extended), jnp.zeros((1, channels), extended.dtype)], axis=0
    )
    pieces = extent // BLOCK
    group = max((g for g in range(1, 17) if pieces % g == 0))
    stride = group * BLOCK
    result = jnp.zeros((weight.shape[2], extent), jnp.float32)

    def advance(turn, current):
        columns = lax.dynamic_slice_in_dim(kernel_map, turn * stride, stride, 1)
        gathered = jnp.take(table, columns, axis=0, mode="clip")
        product = jnp.einsum("kbi,kio->ob", gathered, weight, preferred_element_type=jnp.float32)
        return lax.dynamic_update_slice_in_dim(current, product, turn * stride, 1)

    return lax.fori_loop(0, pieces // group, advance, result)


def route(hidden, outgoing):
    parcel = jnp.transpose(jnp.take(jnp.transpose(hidden), outgoing, axis=0))
    return lax.all_to_all(parcel, ("region", "sub"), split_axis=1, concat_axis=1, tiled=True)


def normalize(conved, active, population, gain, shift):
    masked = jnp.where(active, conved, 0.0)
    average = lax.psum(jnp.sum(masked, axis=1), ("region", "sub")) / population
    offset = jnp.where(active, conved - average[:, None], 0.0)
    spread = lax.psum(jnp.sum(offset * offset, axis=1), ("region", "sub")) / population
    factor = gain * lax.rsqrt(spread + NORM_EPS)
    normed = (conved - average[:, None]) * factor[:, None] + shift[:, None]
    return jnp.where(active, jnp.maximum(normed, 0.0), 0.0).astype(jnp.bfloat16)


def body(
    features, neighbors, send_rows, active_rows, weight_one, weight_two, norm_gain, norm_shift
):
    device = lax.axis_index(("region", "sub"))
    extent = features.shape[1]
    live_count = lax.dynamic_index_in_dim(active_rows, device, keepdims=False)
    active = (jnp.arange(extent, dtype=jnp.int32) < live_count)[None, :]
    population = jnp.sum(active_rows).astype(jnp.float32)
    outgoing = send_rows[0]
    hidden = features
    for depth, weight in enumerate((weight_one, weight_two)):
        arrived = route(hidden, outgoing)
        extended = jnp.concatenate([hidden, arrived], axis=1)
        conved = convolve(extended, neighbors, weight)
        hidden = normalize(conved, active, population, norm_gain[depth], norm_shift[depth])
    return hidden


def solution(mesh):
    placed = (
        P(None, ("region", "sub")),
        P(None, ("region", "sub")),
        P(("region", "sub"), None),
        P(),
        P(),
        P(),
        P(),
        P(),
    )
    return jax.shard_map(
        body, mesh=mesh, in_specs=placed, out_specs=P(None, ("region", "sub")), check_vma=False
    )
```

profile of v0, /device:TPU:0, one launch (start us, length us, event | category | flops | bytes accessed | tf_op | source)
XLA Modules:
  0.0 1933.6 jit_solution(8797046093030034103)
XLA Ops:
  1.5 3.1 copy.61
  4.6 12.1 gather_fusion.2
  16.8 2.9 broadcast_select_fusion.1
  19.6 2.3 copy.59
  22.0 7.4 all-to-all-start
  30.7 1.1 copy.63
  32.4 1.1 copy.68
  33.5 1.3 iota_compare_fusion
  35.4 14.6 all-to-all-done
  50.0 1.6 copy.71
  51.6 9.2 maximum_bitcast_fusion
  61.5 1.9 broadcast.22.clone
  63.4 820.0 %while.26 = (s32[]{:T(128)}, f32[96,8192]{1,0:T(8,128)}, s32[27,8192]{1,0:T(8,128)}, bf16[12289,96]{1,0:T(8,128)(2,1)S(1)}, bf16[27,96,96]{1,2,0:T(8,128)(2,1)},...) while((s32[]{:T(128)}, f32[96,8192]{1,0:T(8,128)}, s32[27,8192]{1,0:T(8,128)}, ...), condition=%wide.region_1.3_spmd, body=%wide.region_0.0_spmd.sunk | while | flops 1019271168 | bytes 38387856 | solution.py:29
  63.4 1.0 constant_dynamic-slice_fusion.4
  65.1 1.0 broadcast_clamp_fusion.4
  66.1 192.0 %gather_fusion = bf16[55296,96]{1,0:T(8,128)(2,1)} fusion(bf16[12289,96]{1,0:T(8,128)(2,1)S(1)} %get-tuple-element.341, s32[55296]{0:T(1024)S(1)} %broadcast_clamp_fusion.4), kind=kCustom, calls=%fused_computation.1.clone.1 | custom fusion | bytes 21454848 | tf_op jit(solution)/shard_map/while/body/eval_jaxpr/jit(_take)/gather | solution.py:25
  258.1 10.4 fusion.17
  268.5 1.0 constant_dynamic-slice_fusion.4
  270.2 1.0 broadcast_clamp_fusion.4
  271.1 192.0 %gather_fusion = bf16[55296,96]{1,0:T(8,128)(2,1)} fusion(bf16[12289,96]{1,0:T(8,128)(2,1)S(1)} %get-tuple-element.341, s32[55296]{0:T(1024)S(1)} %broadcast_clamp_fusion.4), kind=kCustom, calls=%fused_computation.1.clone.1 | custom fusion | bytes 21454848 | tf_op jit(solution)/shard_map/while/body/eval_jaxpr/jit(_take)/gather | solution.py:25
  463.1 10.4 fusion.17
  473.5 1.0 constant_dynamic-slice_fusion.4
  475.2 1.0 broadcast_clamp_fusion.4
  476.1 192.0 %gather_fusion = bf16[55296,96]{1,0:T(8,128)(2,1)} fusion(bf16[12289,96]{1,0:T(8,128)(2,1)S(1)} %get-tuple-element.341, s32[55296]{0:T(1024)S(1)} %broadcast_clamp_fusion.4), kind=kCustom, calls=%fused_computation.1.clone.1 | custom fusion | bytes 21454848 | tf_op jit(solution)/shard_map/while/body/eval_jaxpr/jit(_take)/gather | solution.py:25
  668.1 10.4 fusion.17
  678.5 1.0 constant_dynamic-slice_fusion.4
  680.2 1.0 broadcast_clamp_fusion.4
  681.1 192.0 %gather_fusion = bf16[55296,96]{1,0:T(8,128)(2,1)} fusion(bf16[12289,96]{1,0:T(8,128)(2,1)S(1)} %get-tuple-element.341, s32[55296]{0:T(1024)S(1)} %broadcast_clamp_fusion.4), kind=kCustom, calls=%fused_computation.1.clone.1 | custom fusion | bytes 21454848 | tf_op jit(solution)/shard_map/while/body/eval_jaxpr/jit(_take)/gather | solution.py:25
  873.1 10.4 fusion.17
  883.5 2.4 select_reduce_fusion.1
  885.9 39.1 %psum.28 = f32[96]{0:T(128)S(1)} all-reduce(f32[96]{0:T(128)S(1)} %select_reduce_fusion.1), channel_id=1, replica_groups=mesh['region'=4,'sub'=8] {'region','sub'}, use_global_device_ids=true, to_apply=%region_3.5 | all-reduce | flops 96 | bytes 768 | tf_op jit(solution)/shard_map/psum | solution.py:39
  925.7 40.3 %psum.29 = f32[96]{0:T(128)S(1)} all-reduce(f32[96]{0:T(128)S(1)} %multiply_reduce_fusion.1), channel_id=1, replica_groups=mesh['region'=4,'sub'=8] {'region','sub'}, use_global_device_ids=true, to_apply=%region_6.8 | all-reduce | flops 96 | bytes 768 | tf_op jit(solution)/shard_map/psum | solution.py:41
  966.0 1.8 fusion.7
  967.8 3.9 copy.64
  971.7 16.2 gather_fusion.3
  987.9 4.2 broadcast_select_fusion
  992.1 2.2 copy.65
  994.4 4.6 all-to-all-start.1
  999.0 1.8 select_convert_fusion.1
  1000.8 18.8 all-to-all-done.1
  1019.6 1.2 copy_bitcast_fusion
  1020.8 1.6 maximum_bitcast_fusion.1
  1022.4 2.8 copy.73
  1025.1 2.2 concatenate.15.clone
  1027.4 1.9 broadcast.22
  1029.3 820.1 %while.27 = (s32[]{:T(128)}, f32[96,8192]{1,0:T(8,128)}, s32[27,8192]{1,0:T(8,128)}, bf16[12289,96]{1,0:T(8,128)(2,1)S(1)}, bf16[27,96,96]{1,2,0:T(8,128)(2,1)},...) while((s32[]{:T(128)}, f32[96,8192]{1,0:T(8,128)}, s32[27,8192]{1,0:T(8,128)}, ...), condition=%wide.region_8.10_spmd, body=%wide.region_7.9_spmd.sunk | while | flops 1019271168 | bytes 38387856 | solution.py:29
  1029.3 1.0 constant_dynamic-slice_fusion.5
  1031.0 1.0 broadcast_clamp_fusion.5
  1032.0 192.0 %gather_fusion.1 = bf16[55296,96]{1,0:T(8,128)(2,1)} fusion(bf16[12289,96]{1,0:T(8,128)(2,1)S(1)} %get-tuple-element.368, s32[55296]{0:T(1024)S(1)} %broadcast_clamp_fusion.5), kind=kCustom, calls=%fused_computation.2.clone.1 | custom fusion | bytes 21454848 | tf_op jit(solution)/shard_map/while/body/eval_jaxpr/jit(_take)/gather | solution.py:25
  1224.0 10.4 fusion.20
  1234.3 1.0 constant_dynamic-slice_fusion.5
  1236.0 1.0 broadcast_clamp_fusion.5
  1237.0 192.0 %gather_fusion.1 = bf16[55296,96]{1,0:T(8,128)(2,1)} fusion(bf16[12289,96]{1,0:T(8,128)(2,1)S(1)} %get-tuple-element.368, s32[55296]{0:T(1024)S(1)} %broadcast_clamp_fusion.5), kind=kCustom, calls=%fused_computation.2.clone.1 | custom fusion | bytes 21454848 | tf_op jit(solution)/shard_map/while/body/eval_jaxpr/jit(_take)/gather | solution.py:25
  1429.0 10.4 fusion.20
  1439.4 1.0 constant_dynamic-slice_fusion.5
  1442.1 192.0 %gather_fusion.1 = bf16[55296,96]{1,0:T(8,128)(2,1)} fusion(bf16[12289,96]{1,0:T(8,128)(2,1)S(1)} %get-tuple-element.368, s32[55296]{0:T(1024)S(1)} %broadcast_clamp_fusion.5), kind=kCustom, calls=%fused_computation.2.clone.1 | custom fusion | bytes 21454848 | tf_op jit(solution)/shard_map/while/body/eval_jaxpr/jit(_take)/gather | solution.py:25
  1634.0 10.4 fusion.20
  1644.4 1.0 constant_dynamic-slice_fusion.5
  1647.1 192.0 %gather_fusion.1 = bf16[55296,96]{1,0:T(8,128)(2,1)} fusion(bf16[12289,96]{1,0:T(8,128)(2,1)S(1)} %get-tuple-element.368, s32[55296]{0:T(1024)S(1)} %broadcast_clamp_fusion.5), kind=kCustom, calls=%fused_computation.2.clone.1 | custom fusion | bytes 21454848 | tf_op jit(solution)/shard_map/while/body/eval_jaxpr/jit(_take)/gather | solution.py:25
  1839.0 10.4 fusion.20
  1849.4 2.4 select_reduce_fusion
  1851.8 39.1 %psum.30 = f32[96]{0:T(128)S(1)} all-reduce(f32[96]{0:T(128)S(1)} %select_reduce_fusion), channel_id=1, replica_groups=mesh['region'=4,'sub'=8] {'region','sub'}, use_global_device_ids=true, to_apply=%region_10.12 | all-reduce | flops 96 | bytes 768 | tf_op jit(solution)/shard_map/psum | solution.py:39
  1891.6 40.1 %psum.31 = f32[96]{0:T(128)S(1)} all-reduce(f32[96]{0:T(128)S(1)} %multiply_reduce_fusion), channel_id=1, replica_groups=mesh['region'=4,'sub'=8] {'region','sub'}, use_global_device_ids=true, to_apply=%region_12.14 | all-reduce | flops 96 | bytes 768 | tf_op jit(solution)/shard_map/psum | solution.py:41
  1931.7 1.8 select_convert_fusion
  (54 shorter events, 13.1 us)
Async XLA Ops:
  0.7 16.0 copy-start.6
  1.5 15.3 copy-start.8
  16.7 12.7 copy-start.15
  19.6 11.1 copy-start.2
  19.6 12.8 copy-start.3
  19.6 15.2 copy-start.12
  22.0 28.0 %all-to-all-start = ((bf16[96,32,128]{2,0,1:T(8,128)(2,1)}), bf16[96,32,128]{2,0,1:T(8,128)(2,1)}, u32[]{:S(2)}, u32[]{:S(2)}) async-start(bf16[96,32,128]{2,0,1:T(8,128)(2,1)} %copy.59), calls=%async_computation | async-start | bytes 1572864 | tf_op jit(solution)/shard_map/all_to_all | solution.py:34
  63.4 820.1 %copy-start.4 = (pred[8192]{0:T(1024)(128)(4,1)S(1)}, pred[8192]{0:T(1024)(128)(4,1)}, u32[]{:S(2)}) copy-start(pred[8192]{0:T(1024)(128)(4,1)} %iota_compare_fusion) | copy-start | bytes 24580
  883.5 41.5 %copy-start = (f32[96,8192]{1,0:T(8,128)S(1)}, f32[96,8192]{1,0:T(8,128)}, u32[]{:S(2)}) copy-start(f32[96,8192]{1,0:T(8,128)} %get-tuple-element.194) | copy-start | bytes 9437188
  883.5 82.5 %copy-start.13 = (f32[2,96]{1,0:T(2,128)S(1)}, f32[2,96]{1,0:T(2,128)}, u32[]{:S(2)}) copy-start(f32[2,96]{1,0:T(2,128)} %param.20) | copy-start | bytes 2308
  883.5 82.5 %copy-start.10 = (f32[96]{0:T(128)S(1)}, f32[96]{0:T(128)}, u32[]{:S(2)}) copy-start(f32[96]{0:T(128)} %get-tuple-element.257) | copy-start | bytes 1156
  966.0 5.7 copy-start.7
  971.7 16.2 copy-start.9
  994.4 25.2 %all-to-all-start.1 = ((bf16[96,32,128]{2,0,1:T(8,128)(2,1)}), bf16[96,32,128]{2,0,1:T(8,128)(2,1)}, u32[]{:S(2)}, u32[]{:S(2)}) async-start(bf16[96,32,128]{2,0,1:T(8,128)(2,1)} %copy.65), calls=%async_computation.1 | async-start | bytes 1572864 | tf_op jit(solution)/shard_map/all_to_all | solution.py:34
  1029.3 820.1 %copy-start.5 = (pred[8192]{0:T(1024)(128)(4,1)S(1)}, pred[8192]{0:T(1024)(128)(4,1)}, u32[]{:S(2)}) copy-start(pred[8192]{0:T(1024)(128)(4,1)} %iota_compare_fusion) | copy-start | bytes 24580
  1849.4 41.5 %copy-start.1 = (f32[96,8192]{1,0:T(8,128)S(1)}, f32[96,8192]{1,0:T(8,128)}, u32[]{:S(2)}) copy-start(f32[96,8192]{1,0:T(8,128)} %get-tuple-element.195) | copy-start | bytes 9437188
  1849.4 82.3 %copy-start.14 = (f32[2,96]{1,0:T(2,128)S(1)}, f32[2,96]{1,0:T(2,128)}, u32[]{:S(2)}) copy-start(f32[2,96]{1,0:T(2,128)} %param.20) | copy-start | bytes 2308
  1849.4 82.3 %copy-start.11 = (f32[96]{0:T(128)S(1)}, f32[96]{0:T(128)}, u32[]{:S(2)}) copy-start(f32[96]{0:T(128)} %get-tuple-element.256) | copy-start | bytes 1156
where the time goes:
time: 1940 us; the launch traced here: 1930 us
  local copies, waits for them, and re-layouts  1600 us (82%)
  blocking collectives  159 us (8%)
  matrix products  83.1 us (4%)
  other arithmetic  40.5 us (2%)
  waiting for transfers between devices  33.4 us (2%)
    gather x8, local copies, waits for them, and re-layouts, advance(): gathered = jnp.take(table, columns, axis=0, mode='clip')  1540 us
    dot_general x8, matrix products, advance(): jnp.einsum('kbi,kio->ob', gathered, weight, preferred_element_type=jnp.fl...  83.1 us
    psum x2, blocking collectives, normalize(): lax.psum(jnp.sum(offset * offset, axis=1), ('region', 'sub')) / population  80.5 us
    psum x2, blocking collectives, normalize(): average = lax.psum(jnp.sum(masked, axis=1), ('region', 'sub')) / population  78.2 us
  transfers between devices with their start and end apart: 2, of which 2 were waited for; matrix products, arithmetic and copies ran while one was open for 0% of the time, Pallas kernels for 0%

commit v1 on v0

v1 whole, which is shorter than its diff:
```python
import functools

import jax
import jax.numpy as jnp
from jax import lax
from jax.experimental import pallas as pl
from jax.experimental.pallas import tpu as pltpu
from jax.sharding import PartitionSpec as P

NORM_EPS = 1e-05
LANES = 128
PAD = 8
STEP = 512
GROUP = 16
AXES = ("region", "sub")


def conv_kernel(
    live_ref, index_ref, local_ref, arrived_ref, weight_ref, out_ref, stat_ref, table, staged
):
    step = pl.program_id(0)
    live = live_ref[0]
    rows = local_ref.shape[0]
    halo = arrived_ref.shape[0]
    offsets = index_ref.shape[0]
    middle = offsets // 2

    @pl.when(step == 0)
    def fill():
        zeros = jnp.zeros((PAD, LANES), jnp.float32)
        table[pl.ds(0, PAD), :] = zeros
        table[pl.ds(PAD + rows + halo, PAD), :] = zeros

        def move(source, base):
            def one(turn, carry):
                start = pl.multiple_of(turn * 128, 128)
                table[pl.ds(start + base, 128), :] = source[pl.ds(start, 128), :].astype(
                    jnp.float32
                )
                return carry

            lax.fori_loop(0, source.shape[0] // 128, one, 0)

        move(local_ref, PAD)
        move(arrived_ref, PAD + rows)

    first = step * STEP

    @pl.when(first < live)
    def work():
        sublane = lax.broadcasted_iota(jnp.int32, (8, LANES), 0)

        def collect(turn, carry):
            start = pl.multiple_of(turn * GROUP, GROUP)
            for k in range(offsets):
                if k == middle:
                    block = local_ref[pl.ds(pl.multiple_of(first + start, GROUP), GROUP), :]
                else:
                    halves = []
                    for half in range(GROUP // 8):
                        held = None
                        for s in range(8):
                            place = index_ref[k, start + half * 8 + s] + (PAD - s)
                            window = table[pl.ds(place, 8), :]
                            held = window if s == 0 else jnp.where(sublane == s, window, held)
                        halves.append(held)
                    block = jnp.concatenate(halves, axis=0).astype(jnp.bfloat16)
                staged[pl.ds(start, GROUP), pl.ds(k * LANES, LANES)] = block
            return carry

        lax.fori_loop(0, STEP // GROUP, collect, 0)
        out_ref[pl.ds(pl.multiple_of(first, STEP), STEP), :] = jnp.dot(
            staged[...], weight_ref[...], preferred_element_type=jnp.float32
        )

    @pl.when(step == pl.num_programs(0) - 1)
    def finish():
        blocks = live // LANES

        def total(turn, carry):
            start = pl.multiple_of(turn * LANES, LANES)
            return carry + jnp.sum(out_ref[pl.ds(start, LANES), :], axis=0, keepdims=True)

        summed = lax.fori_loop(0, blocks, total, jnp.zeros((1, LANES), jnp.float32))
        mean = summed / live.astype(jnp.float32)

        def spread(turn, carry):
            start = pl.multiple_of(turn * LANES, LANES)
            offset = out_ref[pl.ds(start, LANES), :] - mean
            return carry + jnp.sum(offset * offset, axis=0, keepdims=True)

        squared = lax.fori_loop(0, blocks, spread, jnp.zeros((1, LANES), jnp.float32))
        row = lax.broadcasted_iota(jnp.int32, (8, LANES), 0)
        stat_ref[...] = jnp.where(row == 0, mean, jnp.where(row == 1, squared, 0.0))


def convolve(live, neighbors, local, arrived, weight):
    offsets, rows = neighbors.shape
    halo = arrived.shape[0]
    whole = lambda shape: pl.BlockSpec(shape, lambda i: (0,) * len(shape))
    return pl.pallas_call(
        conv_kernel,
        grid=(rows // STEP,),
        in_specs=[
            pl.BlockSpec(memory_space=pltpu.SMEM),
            pl.BlockSpec((offsets, STEP), lambda i: (0, i), memory_space=pltpu.SMEM),
            whole((rows, LANES)),
            whole((halo, LANES)),
            whole((offsets * LANES, LANES)),
        ],
        out_specs=[whole((rows, LANES)), whole((8, LANES))],
        out_shape=[
            jax.ShapeDtypeStruct((rows, LANES), jnp.float32),
            jax.ShapeDtypeStruct((8, LANES), jnp.float32),
        ],
        scratch_shapes=[
            pltpu.VMEM((PAD + rows + halo + PAD, LANES), jnp.float32),
            pltpu.VMEM((STEP, offsets * LANES), jnp.bfloat16),
        ],
        compiler_params=pltpu.CompilerParams(vmem_limit_bytes=52 * 1024 * 1024),
        cost_estimate=pl.CostEstimate(
            flops=2 * rows * offsets * LANES * LANES,
            bytes_accessed=rows * LANES * 10,
            transcendentals=0,
        ),
        name="conv",
    )(live, neighbors, local, arrived, weight)


def route(local, outgoing):
    parcel = jnp.take(local, outgoing, axis=0, mode="clip")
    return lax.all_to_all(parcel, AXES, split_axis=0, concat_axis=0, tiled=True)


def widen(weight):
    offsets, fan_in, fan_out = weight.shape
    padded = jnp.pad(weight, ((0, 0), (0, LANES - fan_in), (0, LANES - fan_out)))
    return padded.reshape(offsets * LANES, LANES)


def body(
    features, neighbors, send_rows, active_rows, weight_one, weight_two, norm_gain, norm_shift
):
    device = lax.axis_index(AXES)
    channels, extent = features.shape
    live = lax.dynamic_slice_in_dim(active_rows, device, 1)
    active = (jnp.arange(extent, dtype=jnp.int32) < live[0])[:, None]
    counts = active_rows.astype(jnp.float32)[:, None]
    population = jnp.sum(active_rows).astype(jnp.float32)
    outgoing = send_rows[0]
    local = jnp.pad(jnp.transpose(features), ((0, 0), (0, LANES - channels)))
    fill = ((0, 0), (0, LANES - channels))
    gains = jnp.pad(norm_gain, fill)
    shifts = jnp.pad(norm_shift, fill)
    for depth, weight in enumerate((weight_one, weight_two)):
        arrived = route(local, outgoing)
        conved, stats = convolve(live, neighbors, local, arrived, widen(weight))
        every = lax.all_gather(stats[:2], AXES, axis=0, tiled=False)
        average = jnp.sum(every[:, 0] * counts, axis=0) / population
        apart = every[:, 0] - average
        spread = jnp.sum(every[:, 1] + counts * apart * apart, axis=0) / population
        factor = gains[depth] * lax.rsqrt(spread + NORM_EPS)
        normed = (conved - average) * factor + shifts[depth]
        local = jnp.where(active, jnp.maximum(normed, 0.0), 0.0).astype(jnp.bfloat16)
    return jnp.transpose(local[:, :channels])


def solution(mesh):
    placed = (
        P(None, AXES),
        P(None, AXES),
        P(AXES, None),
        P(),
        P(),
        P(),
        P(),
        P(),
    )
    return jax.shard_map(
        body, mesh=mesh, in_specs=placed, out_specs=P(None, AXES), check_vma=False
    )
```

time: 1940 us -> 840 us (0.43)
  local copies, waits for them, and re-layouts: 1600 us -> 40.2 us
  blocking collectives: 159 us -> 449 us
  Pallas kernels: 0 us -> 276 us
  matrix products: 83.1 us -> 0 us
  other arithmetic: 40.5 us -> 14.9 us
    gather x10 -> x3, local copies, waits for them, and re-layouts: 1560 us -> 28.3 us  [route(): parcel = jnp.take(local, outgoing, axis=0, mode='clip')]
    all_gather x0 -> x2, blocking collectives: none -> 449 us  [body(): every = lax.all_gather(stats[:2], AXES, axis=0, tiled=False)]
    pallas_call x0 -> x2, Pallas kernels: none -> 276 us  [convolve(): pl.pallas_call(conv_kernel, grid=(rows // STEP,), in_specs=[pl.BlockSpec(...]
    psum x4 -> x0, blocking collectives: 159 us -> none  [the longest x2 80.5 us: normalize(): lax.psum(jnp.sum(offset * offset, axis=1), ('region', 'sub')) / population]
    dot_general x8 -> x0, matrix products: 83.1 us -> none  [advance(): jnp.einsum('kbi,kio->ob', gathered, weight, preferred_element_type=jnp.fl...]
  transfers between devices with their start and end apart: 2 -> 2, of which waited for: 2 -> 2; matrix products, arithmetic and copies ran while one was open for 0% -> 1% of each run, Pallas kernels for 0% -> 0%
where the time goes in v1:
time: 840 us; the launch traced here: 837 us
  blocking collectives  449 us (53%)
  Pallas kernels  276 us (33%)
  waiting for transfers between devices  45.5 us (5%)
  local copies, waits for them, and re-layouts  40.2 us (5%)
  other arithmetic  14.9 us (2%)
  starting transfers between devices  10.1 us (1%)
    all_gather x2, blocking collectives, body(): every = lax.all_gather(stats[:2], AXES, axis=0, tiled=False)  449 us
    pallas_call x2, Pallas kernels, convolve(): pl.pallas_call(conv_kernel, grid=(rows // STEP,), in_specs=[pl.BlockSpec(...  276 us
    all_to_all x2, waiting for transfers between devices, route(): return lax.all_to_all(parcel, AXES, split_axis=0, concat_axis=0, tiled=True)  45.5 us
    gather x3, local copies, waits for them, and re-layouts, route(): parcel = jnp.take(local, outgoing, axis=0, mode='clip')  28.3 us
  transfers between devices with their start and end apart: 2, of which 2 were waited for; matrix products, arithmetic and copies ran while one was open for 1% of the time, Pallas kernels for 0%

profile of v1, /device:TPU:0, one launch (start us, length us, event | category | flops | bytes accessed | tf_op | source)
XLA Modules:
  0.0 836.8 jit_solution(6892366695553389329)
XLA Ops:
  0.0 3.1 copy.12
  3.1 0.7 broadcast_clamp_fusion
  3.8 12.1 %gather_fusion = bf16[4096,96]{1,0:T(8,128)(2,1)S(1)} fusion(bf16[8192,96]{1,0:T(8,128)(2,1)S(1)} %bitcast.46, s32[4096]{0:T(1024)S(1)} %broadcast_clamp_fusion), kind=kCustom, calls=%fused_computation | custom fusion | bytes 1589248 | tf_op jit(solution)/shard_map/jit(_take)/gather | solution.py:131
  16.0 1.2 gather.11
  17.1 0.0 copy-start.5
  17.1 0.0 copy-start.4
  17.1 0.0 copy-start
  17.1 7.4 all-to-all-start
  24.6 1.7 pad.19.local_ref
  26.3 1.3 pad.20
  27.6 0.0 copy-done.5
  27.6 0.6 dynamic_slice.3.live_ref
  28.3 0.7 fusion.18
  29.6 0.0 copy-done.4
  29.6 0.6 iota_compare_fusion
  30.2 20.6 %all-to-all-done = bf16[32,128,128]{2,1,0:T(8,128)(2,1)} async-done(((bf16[32,128,128]{2,1,0:T(8,128)(2,1)}), bf16[32,128,128]{2,1,0:T(8,128)(2,1)}, u32[]{:S(2)}, u32[]{:S(2)}) %all-to-all-start) | async-done | bytes 1048608 | tf_op jit(solution)/shard_map/all_to_all | solution.py:132
  50.8 0.0 copy-done
  50.8 0.0 copy-start.3
  50.8 138.0 %conv.2 = (f32[8192,128]{1,0:T(8,128)}, f32[8,128]{1,0:T(8,128)S(1)}) custom-call(s32[1]{0:T(128)} %dynamic_slice.3.live_ref, s32[27,8192]{1,0:T(8,128)S(1)} %copy-done, bf16[8192,128]{1,0:T(8,128)(2,1)} %pad.19.local_ref, bf16[4096,128]{1,0:T(8,128)(2,1)} %bitcast.4.arrived_ref, bf16[3456,128]{1,0:T(8,128)(2,1)S(1)} %bitcast.44), custom_call_target="tpu_custom_call" | custom-call | flops 7247757312 | bytes 10485760 | tf_op jit(solution)/shard_map/conv/pallas_call | solution.py:101
  188.8 224.8 %all-gather.2 = f32[32,2,128]{2,1,0:T(2,128)S(1)} all-gather(f32[1,2,128]{2,1,0:T(2,128)S(1)} %slice_bitcast_fusion.1), channel_id=2, replica_groups=mesh['region'=4,'sub'=8] {'region','sub'}, dimensions={0}, use_global_device_ids=true | all-gather | bytes 33792 | tf_op jit(solution)/shard_map/all_gather | solution.py:158
  413.6 0.1 multiply_reduce_fusion.1
  413.7 0.1 fusion.7
  413.8 0.0 copy-done.3
  413.8 6.2 select_convert_fusion.local_ref
  420.1 0.0 copy-start.1
  420.1 15.0 %gather_fusion.1 = bf16[4096,128]{1,0:T(8,128)(2,1)} fusion(bf16[8192,128]{1,0:T(8,128)(2,1)S(1)} %select_convert_fusion.local_ref, s32[4096]{0:T(1024)S(1)} %broadcast_clamp_fusion), kind=kCustom, calls=%fused_computation.1 | custom fusion | bytes 2113536 | tf_op jit(solution)/shard_map/jit(_take)/gather | solution.py:131
  435.1 0.0 copy-done.1
  435.1 2.6 all-to-all-start.1
  437.8 1.3 pad.23
  439.1 24.9 %all-to-all-done.1 = bf16[32,128,128]{2,1,0:T(8,128)(2,1)S(1)} async-done(((bf16[32,128,128]{2,1,0:T(8,128)(2,1)}), bf16[32,128,128]{2,1,0:T(8,128)(2,1)S(1)}, u32[]{:S(2)}, u32[]{:S(2)}) %all-to-all-start.1) | async-done | bytes 1048608 | tf_op jit(solution)/shard_map/all_to_all | solution.py:132
  464.0 0.0 copy-start.2
  464.0 1.0 copy-done.2
  465.0 138.0 %conv.3 = (f32[8192,128]{1,0:T(8,128)}, f32[8,128]{1,0:T(8,128)S(1)}) custom-call(s32[1]{0:T(128)} %dynamic_slice.3.live_ref, s32[27,8192]{1,0:T(8,128)S(1)} %copy-done, bf16[8192,128]{1,0:T(8,128)(2,1)} %copy-done.1, bf16[4096,128]{1,0:T(8,128)(2,1)} %bitcast.50, bf16[3456,128]{1,0:T(8,128)(2,1)S(1)} %bitcast.45), custom_call_target="tpu_custom_call" | custom-call | flops 7247757312 | bytes 10485760 | tf_op jit(solution)/shard_map/conv/pallas_call | solution.py:101
  602.9 224.6 %all-gather.3 = f32[32,2,128]{2,1,0:T(2,128)S(1)} all-gather(f32[1,2,128]{2,1,0:T(2,128)S(1)} %slice_bitcast_fusion), channel_id=3, replica_groups=mesh['region'=4,'sub'=8] {'region','sub'}, dimensions={0}, use_global_device_ids=true | all-gather | bytes 33792 | tf_op jit(solution)/shard_map/all_gather | solution.py:158
  827.6 0.1 multiply_reduce_fusion
  827.7 0.1 fusion.9
  827.8 6.2 fusion.5
  834.1 2.8 copy.16
  (9 shorter events, 0.1 us)
Async XLA Ops:
  17.1 10.5 %copy-start.5 = (s32[32]{0:T(128)S(1)}, s32[32]{0:T(128)}, u32[]{:S(2)}) copy-start(s32[32]{0:T(128)} %param.11) | copy-start | bytes 388
  17.1 12.4 %copy-start.4 = (f32[2,96]{1,0:T(2,128)S(1)}, f32[2,96]{1,0:T(2,128)}, u32[]{:S(2)}) copy-start(f32[2,96]{1,0:T(2,128)} %param.15) | copy-start | bytes 2308
  17.1 33.7 %copy-start = (s32[27,8192]{1,0:T(8,128)S(1)}, s32[27,8192]{1,0:T(8,128)}, u32[]{:S(2)}) copy-start(s32[27,8192]{1,0:T(8,128)} %index_ref.3) | copy-start | bytes 2654212
  17.1 33.6 %all-to-all-start = ((bf16[32,128,128]{2,1,0:T(8,128)(2,1)}), bf16[32,128,128]{2,1,0:T(8,128)(2,1)}, u32[]{:S(2)}, u32[]{:S(2)}) async-start(bf16[32,128,128]{2,1,0:T(8,128)(2,1)} %bitcast.49), calls=%async_computation | async-start | bytes 2097152 | tf_op jit(solution)/shard_map/all_to_all | solution.py:132
  50.8 363.0 %copy-start.3 = (f32[2,96]{1,0:T(2,128)S(1)}, f32[2,96]{1,0:T(2,128)}, u32[]{:S(2)}) copy-start(f32[2,96]{1,0:T(2,128)} %param.14) | copy-start | bytes 2308
  420.1 15.0 %copy-start.1 = (bf16[8192,128]{1,0:T(8,128)(2,1)}, bf16[8192,128]{1,0:T(8,128)(2,1)S(1)}, u32[]{:S(2)}) copy-start(bf16[8192,128]{1,0:T(8,128)(2,1)S(1)} %select_convert_fusion.local_ref) | copy-start | bytes 6291460
  435.1 28.9 %all-to-all-start.1 = ((bf16[32,128,128]{2,1,0:T(8,128)(2,1)}), bf16[32,128,128]{2,1,0:T(8,128)(2,1)S(1)}, u32[]{:S(2)}, u32[]{:S(2)}) async-start(bf16[32,128,128]{2,1,0:T(8,128)(2,1)} %bitcast.48), calls=%async_computation.1 | async-start | bytes 2097152 | tf_op jit(solution)/shard_map/all_to_all | solution.py:132
  464.0 1.0 copy-start.2

commit v2 on v1

v2 whole, which is shorter than its diff:
```python
import functools

import jax
import jax.numpy as jnp
from jax import lax
from jax.experimental import pallas as pl
from jax.experimental.pallas import tpu as pltpu
from jax.sharding import PartitionSpec as P

NORM_EPS = 1e-05
LANES = 128
PAD = 8
BLOCK = 128
LEAST = 2048
STEP = 512
GROUP = 16
AXES = ("region", "sub")
MESH = pl.DeviceIdType.MESH


def conv_kernel(
    job_ref, index_ref, local_ref, arrived_ref, weight_ref, out_ref, stat_ref, table, staged
):
    step = pl.program_id(0)
    live = job_ref[0]
    base = job_ref[1]
    rows = local_ref.shape[0]
    halo = arrived_ref.shape[0]
    offsets = index_ref.shape[0]
    middle = offsets // 2

    @pl.when((step == 0) & (live > 0))
    def fill():
        zeros = jnp.zeros((PAD, LANES), jnp.float32)
        table[pl.ds(0, PAD), :] = zeros
        table[pl.ds(PAD + rows + halo, PAD), :] = zeros

        def move(source, base):
            def one(turn, carry):
                start = pl.multiple_of(turn * 128, 128)
                table[pl.ds(start + base, 128), :] = source[pl.ds(start, 128), :].astype(
                    jnp.float32
                )
                return carry

            lax.fori_loop(0, source.shape[0] // 128, one, 0)

        move(local_ref, PAD)
        move(arrived_ref, PAD + rows)

    first = step * STEP

    @pl.when(first < live)
    def work():
        sublane = lax.broadcasted_iota(jnp.int32, (8, LANES), 0)

        def collect(turn, carry):
            start = pl.multiple_of(turn * GROUP, GROUP)
            for k in range(offsets):
                if k == middle:
                    own = pl.multiple_of(base + first + start, GROUP)
                    block = local_ref[pl.ds(own, GROUP), :]
                else:
                    halves = []
                    for half in range(GROUP // 8):
                        held = None
                        for s in range(8):
                            place = index_ref[k, start + (half * 8 + s)]
                            window = table[pl.ds(place, 8), :]
                            held = window if s == 0 else jnp.where(sublane == s, window, held)
                        halves.append(held)
                    block = jnp.concatenate(halves, axis=0).astype(jnp.bfloat16)
                staged[pl.ds(start, GROUP), pl.ds(k * LANES, LANES)] = block
            return carry

        lax.fori_loop(0, jnp.minimum(STEP, live - first) // GROUP, collect, 0)
        out_ref[pl.ds(pl.multiple_of(first, STEP), STEP), :] = jnp.dot(
            staged[...], weight_ref[...], preferred_element_type=jnp.float32
        )

    @pl.when(step == pl.num_programs(0) - 1)
    def finish():
        blocks = live // LANES

        def total(turn, carry):
            start = pl.multiple_of(turn * LANES, LANES)
            return carry + jnp.sum(out_ref[pl.ds(start, LANES), :], axis=0, keepdims=True)

        summed = lax.fori_loop(0, blocks, total, jnp.zeros((1, LANES), jnp.float32))
        mean = summed / jnp.maximum(live, 1).astype(jnp.float32)

        def spread(turn, carry):
            start = pl.multiple_of(turn * LANES, LANES)
            offset = out_ref[pl.ds(start, LANES), :] - mean
            return carry + jnp.sum(offset * offset, axis=0, keepdims=True)

        squared = lax.fori_loop(0, blocks, spread, jnp.zeros((1, LANES), jnp.float32))
        row = lax.broadcasted_iota(jnp.int32, (8, LANES), 0)
        stat_ref[...] = jnp.where(row == 0, mean, jnp.where(row == 1, squared, 0.0))


def convolve(job, indices, local, arrived, weight, room):
    offsets, rows = indices.shape
    extent = local.shape[0]
    halo = arrived.shape[0]
    whole = lambda shape: pl.BlockSpec(shape, lambda i, job: (0,) * len(shape))

    def columns(i, job):
        return (0, jnp.minimum(i, jnp.maximum(job[0] - 1, 0) // STEP))

    return pl.pallas_call(
        conv_kernel,
        grid_spec=pltpu.PrefetchScalarGridSpec(
            num_scalar_prefetch=1,
            grid=(rows // STEP,),
            in_specs=[
                pl.BlockSpec((offsets, STEP), columns, memory_space=pltpu.SMEM),
                whole((extent, LANES)),
                whole((halo, LANES)),
                whole((offsets * LANES, LANES)),
            ],
            out_specs=[whole((rows + room, LANES)), whole((8, LANES))],
            scratch_shapes=[
                pltpu.VMEM((PAD + extent + halo + PAD, LANES), jnp.float32),
                pltpu.VMEM((STEP, offsets * LANES), jnp.bfloat16),
            ],
        ),
        out_shape=[
            jax.ShapeDtypeStruct((rows + room, LANES), jnp.float32),
            jax.ShapeDtypeStruct((8, LANES), jnp.float32),
        ],
        compiler_params=pltpu.CompilerParams(vmem_limit_bytes=56 * 1024 * 1024),
        cost_estimate=pl.CostEstimate(
            flops=20 * rows * offsets * LANES * LANES,
            bytes_accessed=rows * LANES * 100,
            transcendentals=0,
        ),
        name="conv",
    )(job, indices, local, arrived, weight)


def share_kernel(regions, subs, mine_ref, every_ref, send_sem, recv_sem):
    devices = regions * subs
    me = lax.axis_index("region") * subs + lax.axis_index("sub")
    place = lambda p: (lax.div(p, subs), lax.rem(p, subs))
    barrier = pltpu.get_barrier_semaphore()

    def greet(off, carry):
        other = lax.rem(me + off, devices)
        pl.semaphore_signal(barrier, inc=1, device_id=place(other), device_id_type=MESH)
        return carry

    lax.fori_loop(1, devices, greet, 0)
    pl.semaphore_wait(barrier, devices - 1)

    def copy(off, slot):
        return pltpu.make_async_remote_copy(
            src_ref=mine_ref,
            dst_ref=every_ref.at[slot],
            send_sem=send_sem.at[off],
            recv_sem=recv_sem.at[off],
            device_id=place(lax.rem(me + off, devices)),
            device_id_type=MESH,
        )

    def send(off, carry):
        copy(off, me).start()
        return carry

    def finish(off, carry):
        copy(off, me).wait_send()
        copy(off, lax.rem(me + devices - off, devices)).wait_recv()
        return carry

    lax.fori_loop(1, devices, send, 0)
    every_ref[me] = mine_ref[...]
    lax.fori_loop(1, devices, finish, 0)


def share(mine, regions, subs):
    devices = regions * subs
    return pl.pallas_call(
        functools.partial(share_kernel, regions, subs),
        out_shape=jax.ShapeDtypeStruct((devices,) + mine.shape, mine.dtype),
        in_specs=[pl.BlockSpec(memory_space=pltpu.VMEM)],
        out_specs=pl.BlockSpec(memory_space=pltpu.VMEM),
        scratch_shapes=[
            pltpu.SemaphoreType.DMA((devices,)),
            pltpu.SemaphoreType.DMA((devices,)),
        ],
        compiler_params=pltpu.CompilerParams(collective_id=0, has_side_effects=True),
        name="share",
    )(mine)


def route(local, outgoing):
    parcel = jnp.take(local, outgoing, axis=0, mode="clip")
    return lax.all_to_all(parcel, AXES, split_axis=0, concat_axis=0, tiled=True)


def widen(weight):
    offsets, fan_in, fan_out = weight.shape
    padded = jnp.pad(weight, ((0, 0), (0, LANES - fan_in), (0, LANES - fan_out)))
    return padded.reshape(offsets * LANES, LANES)


def body(
    regions,
    subs,
    features,
    neighbors,
    send_rows,
    active_rows,
    weight_one,
    weight_two,
    norm_gain,
    norm_shift,
):
    device = lax.axis_index(AXES)
    channels, extent = features.shape
    reach = (extent - LEAST) // 2
    pairs = [(s, s ^ 1) for s in range(subs)]
    swap = lambda value: lax.ppermute(value, "sub", pairs)
    live = active_rows[device]
    active = (jnp.arange(extent, dtype=jnp.int32) < live)[:, None]
    population = jnp.sum(active_rows).astype(jnp.float32)
    twin_rows = active_rows.reshape(-1, 2)[:, ::-1].reshape(-1)
    given_rows = jnp.maximum(active_rows - twin_rows, 0) // (2 * BLOCK) * BLOCK
    taken_rows = given_rows.reshape(-1, 2)[:, ::-1].reshape(-1)
    kept_rows = active_rows - given_rows
    kept = kept_rows[device]
    taken = taken_rows[device]
    counts = jnp.stack([kept_rows, taken_rows], axis=1).astype(jnp.float32)[:, :, None]
    outgoing = send_rows[0]
    local = jnp.pad(jnp.transpose(features), ((0, 0), (0, LANES - channels)))
    indices = neighbors + (PAD - jnp.arange(extent, dtype=jnp.int32) % 8)[None, :]
    handed = lax.dynamic_slice_in_dim(jnp.pad(indices, ((0, 0), (0, reach))), kept, reach, 1)
    borrowed = swap(handed)
    own_job = jnp.stack([kept, jnp.zeros_like(kept)])
    twin_job = jnp.stack([taken, kept_rows[device ^ 1]])
    fill = ((0, 0), (0, LANES - channels))
    gains = jnp.pad(norm_gain, fill)
    shifts = jnp.pad(norm_shift, fill)
    for depth, weight in enumerate((weight_one, weight_two)):
        wide = widen(weight)
        arrived = route(local, outgoing)
        twin_local = swap(local)
        twin_arrived = swap(arrived)
        conved, own_stats = convolve(own_job, indices, local, arrived, wide, reach)
        helped, twin_stats = convolve(twin_job, borrowed, twin_local, twin_arrived, wide, 0)
        returned = swap(helped)
        mine = jnp.concatenate([own_stats[:2], twin_stats[:2], jnp.zeros_like(own_stats[:4])])
        every = share(mine, regions, subs)
        means, squares = every[:, 0:4:2], every[:, 1:4:2]
        average = jnp.sum(means * counts, axis=(0, 1)) / population
        apart = means - average
        spread = jnp.sum(squares + counts * apart * apart, axis=(0, 1)) / population
        factor = gains[depth] * lax.rsqrt(spread + NORM_EPS)
        conved = lax.dynamic_update_slice_in_dim(conved, returned, kept, 0)[:extent]
        normed = (conved - average) * factor + shifts[depth]
        local = jnp.where(active, jnp.maximum(normed, 0.0), 0.0).astype(jnp.bfloat16)
    return jnp.transpose(local[:, :channels])


def solution(mesh):
    placed = (
        P(None, AXES),
        P(None, AXES),
        P(AXES, None),
        P(),
        P(),
        P(),
        P(),
        P(),
    )
    return jax.shard_map(
        functools.partial(body, mesh.shape["region"], mesh.shape["sub"]),
        mesh=mesh,
        in_specs=placed,
        out_specs=P(None, AXES),
        check_vma=False,
    )
```

time: 840 us -> 846 us (level)
  blocking collectives: 449 us -> 0 us
  Pallas kernels: 276 us -> 695 us
  local copies, waits for them, and re-layouts: 40.2 us -> 64.7 us
    all_gather x2 -> x0, blocking collectives: 449 us -> none  [body(): every = lax.all_gather(stats[:2], AXES, axis=0, tiled=False)]
    pallas_call x2 -> x6, Pallas kernels: 276 us -> 695 us  [the longest x2 477 us: share(): pl.pallas_call(functools.partial(share_kernel, regions, subs), out_shape=...]
    dynamic_update_slice x0 -> x2, local copies, waits for them, and re-layouts: none -> 10.6 us  [body(): conved = lax.dynamic_update_slice_in_dim(conved, returned, kept, 0)[:extent]]
    slice x2 -> x9, local copies, waits for them, and re-layouts: 0.05 us -> 8.81 us  [the longest x4 3.65 us: body(): means, squares = (every[:, 0:4:2], every[:, 1:4:2])]
  transfers between devices with their start and end apart: 2 -> 9, of which waited for: 2 -> 2; matrix products, arithmetic and copies ran while one was open for 1% -> 3% of each run, Pallas kernels for 0% -> 78%
where the time goes in v2:
time: 846 us; the launch traced here: 843 us
  Pallas kernels  695 us (82%)
  local copies, waits for them, and re-layouts  64.7 us (8%)
  waiting for transfers between devices  50.2 us (6%)
  other arithmetic  17.5 us (2%)
  starting transfers between devices  12.9 us (2%)
    pallas_call x2, Pallas kernels, share(): pl.pallas_call(functools.partial(share_kernel, regions, subs), out_shape=...  477 us
    pallas_call x4, Pallas kernels, convolve(): pl.pallas_call(conv_kernel, grid_spec=pltpu.PrefetchScalarGridSpec(num_sc...  219 us
    all_to_all x2, waiting for transfers between devices, route(): return lax.all_to_all(parcel, AXES, split_axis=0, concat_axis=0, tiled=True)  50.2 us
    gather x3, local copies, waits for them, and re-layouts, route(): parcel = jnp.take(local, outgoing, axis=0, mode='clip')  28.3 us
  transfers between devices with their start and end apart: 9, of which 2 were waited for; matrix products, arithmetic and copies ran while one was open for 3% of the time, Pallas kernels for 78%

profile of v2, /device:TPU:0, one launch (start us, length us, event | category | flops | bytes accessed | tf_op | source)
XLA Modules:
  0.0 843.4 jit_solution(8545415348783952481)
XLA Ops:
  0.0 3.1 copy.12
  3.1 0.7 broadcast_clamp_fusion
  3.8 12.1 %gather_fusion = bf16[4096,96]{1,0:T(8,128)(2,1)S(1)} fusion(bf16[8192,96]{1,0:T(8,128)(2,1)S(1)} %bitcast.32, s32[4096]{0:T(1024)S(1)} %broadcast_clamp_fusion), kind=kCustom, calls=%fused_computation | custom fusion | bytes 1589248 | tf_op jit(solution)/shard_map/jit(_take)/gather | solution.py:197
  16.0 1.2 gather.11
  17.1 7.4 all-to-all-start
  24.6 1.7 pad.23.local_ref
  26.3 0.2 collective-permute-start.1
  26.5 24.3 %all-to-all-done = bf16[32,128,128]{2,1,0:T(8,128)(2,1)} async-done(((bf16[32,128,128]{2,1,0:T(8,128)(2,1)}), bf16[32,128,128]{2,1,0:T(8,128)(2,1)}, u32[]{:S(2)}, u32[]{:S(2)}) %all-to-all-start) | async-done | bytes 1048608 | tf_op jit(solution)/shard_map/all_to_all | solution.py:198
  50.8 0.1 broadcast_add_fusion.index_ref
  50.9 0.1 reshape.102
  51.0 0.1 rev.6
  51.1 0.1 reshape.103
  51.2 0.6 fusion.26
  51.8 0.6 fusion.28
  54.3 0.2 pad_dynamic-slice_fusion
  54.5 0.6 collective-permute-start
  55.1 0.1 reshape.105
  55.1 0.1 rev.7
  55.2 0.1 reshape.106
  55.3 0.1 stack.17
  55.4 0.6 dynamic_slice.15
  56.0 2.2 pad.24
  58.3 0.6 dynamic_slice.17
  58.9 0.1 copy.13
  59.6 0.1 pad.36.clone
  59.7 1.3 pad_add_fusion.job_ref
  61.0 1.8 pad_add_fusion.1.job_ref
  62.8 0.6 iota_compare_fusion
  63.4 0.7 copy-done.8
  64.2 20.7 %conv.5 = (f32[3072,128]{1,0:T(8,128)}, f32[8,128]{1,0:T(8,128)}) custom-call(s32[2]{0:T(128)} %pad_add_fusion.1.job_ref, s32[27,3072]{1,0:T(8,128)} %copy-done.8, bf16[8192,128]{1,0:T(8,128)(2,1)} %collective-permute-done.1.local_ref, bf16[4096,128]{1,0:T(8,128)(2,1)} %collective-permute-done.2.arrived_ref, bf16[3456,128]{1,0:T(8,128)(2,1)} %bitcast.37), custom_call_target="tpu_custom_call" | custom-call | flops 27179089920 | bytes 39321600 | tf_op jit(solution)/shard_map/conv/pallas_call | solution.py:111
  84.9 0.0 copy-start.6
  84.9 0.1 collective-permute-start.3
  85.0 88.7 %conv.4 = (f32[11264,128]{1,0:T(8,128)}, f32[8,128]{1,0:T(8,128)}) custom-call(s32[2]{0:T(128)} %pad_add_fusion.job_ref, s32[27,8192]{1,0:T(8,128)} %copy-done.1, bf16[8192,128]{1,0:T(8,128)(2,1)} %pad.23.local_ref, bf16[4096,128]{1,0:T(8,128)(2,1)} %bitcast.4.arrived_ref, bf16[3456,128]{1,0:T(8,128)(2,1)} %bitcast.38), custom_call_target="tpu_custom_call" | custom-call | flops 72477573120 | bytes 104857600 | tf_op jit(solution)/shard_map/conv/pallas_call | solution.py:111
  173.6 0.7 slice.46
  174.3 0.7 slice.47
  175.0 0.7 maximum_maximum_fusion.mine_ref
  175.6 238.2 %share.2 = f32[32,8,128]{2,1,0:T(8,128)} custom-call(f32[8,128]{1,0:T(8,128)} %maximum_maximum_fusion.mine_ref), custom_call_target="tpu_custom_call" | custom-call | tf_op jit(solution)/shard_map/share/pallas_call | solution.py:182
  413.8 0.9 slice.50
  414.8 0.9 slice.48
  415.7 0.1 multiply_reduce_fusion.1
  415.8 0.1 fusion.17
  416.0 5.3 dynamic_update_slice.6
  421.3 6.2 fusion.9.local_ref
  427.6 15.0 %gather_fusion.1 = bf16[4096,128]{1,0:T(8,128)(2,1)} fusion(bf16[8192,128]{1,0:T(8,128)(2,1)S(1)} %fusion.9.local_ref, s32[4096]{0:T(1024)S(1)} %broadcast_clamp_fusion), kind=kCustom, calls=%fused_computation.1 | custom fusion | bytes 2113536 | tf_op jit(solution)/shard_map/jit(_take)/gather | solution.py:197
  442.6 4.5 all-to-all-start.1
  447.1 0.1 collective-permute-start.4
  447.2 25.9 %all-to-all-done.1 = bf16[32,128,128]{2,1,0:T(8,128)(2,1)S(1)} async-done(((bf16[32,128,128]{2,1,0:T(8,128)(2,1)}), bf16[32,128,128]{2,1,0:T(8,128)(2,1)S(1)}, u32[]{:S(2)}, u32[]{:S(2)}) %all-to-all-start.1) | async-done | bytes 1048608 | tf_op jit(solution)/shard_map/all_to_all | solution.py:198
  473.1 2.6 pad.28
  475.7 0.0 collective-permute-done.5.arrived_ref
  475.8 1.0 copy-done.7
  476.7 20.7 %conv.7 = (f32[3072,128]{1,0:T(8,128)}, f32[8,128]{1,0:T(8,128)}) custom-call(s32[2]{0:T(128)} %pad_add_fusion.1.job_ref, s32[27,3072]{1,0:T(8,128)} %copy-done.8, bf16[8192,128]{1,0:T(8,128)(2,1)} %collective-permute-done.4.local_ref, bf16[4096,128]{1,0:T(8,128)(2,1)} %copy-done.7, bf16[3456,128]{1,0:T(8,128)(2,1)} %bitcast.39), custom_call_target="tpu_custom_call" | custom-call | flops 27179089920 | bytes 39321600 | tf_op jit(solution)/shard_map/conv/pallas_call | solution.py:111
  497.5 88.6 %conv.6 = (f32[11264,128]{1,0:T(8,128)}, f32[8,128]{1,0:T(8,128)}) custom-call(s32[2]{0:T(128)} %pad_add_fusion.job_ref, s32[27,8192]{1,0:T(8,128)} %copy-done.1, bf16[8192,128]{1,0:T(8,128)(2,1)} %copy-done, bf16[4096,128]{1,0:T(8,128)(2,1)} %bitcast.36, bf16[3456,128]{1,0:T(8,128)(2,1)} %bitcast.40), custom_call_target="tpu_custom_call" | custom-call | flops 72477573120 | bytes 104857600 | tf_op jit(solution)/shard_map/conv/pallas_call | solution.py:111
  586.1 0.7 slice.53
  586.8 0.7 slice.54
  587.5 0.7 maximum_maximum_fusion.1.mine_ref
  588.1 238.3 %share.3 = f32[32,8,128]{2,1,0:T(8,128)} custom-call(f32[8,128]{1,0:T(8,128)} %maximum_maximum_fusion.1.mine_ref), custom_call_target="tpu_custom_call" | custom-call | tf_op jit(solution)/shard_map/share/pallas_call | solution.py:182
  826.5 0.9 slice.57
  827.4 0.9 slice.55
  828.3 0.1 multiply_reduce_fusion
  828.4 0.1 fusion.16
  828.6 5.3 dynamic_update_slice.7
  833.9 2.5 slice.65
  836.3 4.3 fusion.10
  840.6 2.8 copy.14
  (31 shorter events, 0.1 us)
Async XLA Ops:
  17.1 33.7 %copy-start.2 = (s32[27,8192]{1,0:T(8,128)S(1)}, s32[27,8192]{1,0:T(8,128)}, u32[]{:S(2)}) copy-start(s32[27,8192]{1,0:T(8,128)} %param.9) | copy-start | bytes 2654212
  17.1 33.8 %copy-start.5 = (s32[32]{0:T(128)S(1)}, s32[32]{0:T(128)}, u32[]{:S(2)}) copy-start(s32[32]{0:T(128)} %param.11) | copy-start | bytes 388
  17.1 33.6 %all-to-all-start = ((bf16[32,128,128]{2,1,0:T(8,128)(2,1)}), bf16[32,128,128]{2,1,0:T(8,128)(2,1)}, u32[]{:S(2)}, u32[]{:S(2)}) async-start(bf16[32,128,128]{2,1,0:T(8,128)(2,1)} %bitcast.34), calls=%async_computation | async-start | bytes 2097152 | tf_op jit(solution)/shard_map/all_to_all | solution.py:198
  26.3 37.1 %collective-permute-start.1 = (bf16[8192,128]{1,0:T(8,128)(2,1)}, bf16[8192,128]{1,0:T(8,128)(2,1)}, u32[]{:S(2)}, u32[]{:S(2)}) collective-permute-start(bf16[8192,128]{1,0:T(8,128)(2,1)} %pad.23.local_ref), channel_id=1, source_target_pairs={{0,1},{1,0},{2,3},{3,2},{4,5},{5,4},{6,7},{7,6},{8,9},{9,8},{10,11... | collective-permute-start | bytes 6291464 | tf_op jit(solution)/shard_map/ppermute | solution.py:223
  50.8 12.6 %collective-permute-start.2 = (bf16[4096,128]{1,0:T(8,128)(2,1)}, bf16[4096,128]{1,0:T(8,128)(2,1)}, u32[]{:S(2)}, u32[]{:S(2)}) collective-permute-start(bf16[4096,128]{1,0:T(8,128)(2,1)} %bitcast.4.arrived_ref), channel_id=1, source_target_pairs={{0,1},{1,0},{2,3},{3,2},{4,5},{5,4},{6,7},{7,6},{8,9},{9,8},{10,11... | collective-permute-start | bytes 3145736 | tf_op jit(solution)/shard_map/ppermute | solution.py:223
  50.9 34.0 %copy-start.1 = (s32[27,8192]{1,0:T(8,128)}, s32[27,8192]{1,0:T(8,128)S(1)}, u32[]{:S(2)}) copy-start(s32[27,8192]{1,0:T(8,128)S(1)} %broadcast_add_fusion.index_ref) | copy-start | bytes 2654212
  54.5 8.9 %collective-permute-start = (s32[27,3072]{1,0:T(8,128)S(1)}, s32[27,3072]{1,0:T(8,128)S(1)}, u32[]{:S(2)}, u32[]{:S(2)}) collective-permute-start(s32[27,3072]{1,0:T(8,128)S(1)} %pad_dynamic-slice_fusion), channel_id=1, source_target_pairs={{0,1},{1,0},{2,3},{3,2},{4,5},{5,4},{6,7},{7,6},{8,9},{9,8},{10,11... | collective-permute-start | bytes 995336 | tf_op jit(solution)/shard_map/ppermute | solution.py:223
  63.4 0.8 copy-start.8
  84.9 331.1 %copy-start.4 = (f32[2,96]{1,0:T(2,128)S(1)}, f32[2,96]{1,0:T(2,128)}, u32[]{:S(2)}) copy-start(f32[2,96]{1,0:T(2,128)} %param.14) | copy-start | bytes 2308
  84.9 331.1 %copy-start.6 = (f32[2,96]{1,0:T(2,128)S(1)}, f32[2,96]{1,0:T(2,128)}, u32[]{:S(2)}) copy-start(f32[2,96]{1,0:T(2,128)} %param.15) | copy-start | bytes 2308
  84.9 331.1 %collective-permute-start.3 = (f32[3072,128]{1,0:T(8,128)}, f32[3072,128]{1,0:T(8,128)S(1)}, u32[]{:S(2)}, u32[]{:S(2)}) collective-permute-start(f32[3072,128]{1,0:T(8,128)} %get-tuple-element.14), channel_id=1, source_target_pairs={{0,1},{1,0},{2,3},{3,2},{4,5},{5,4},{6,7},{7,6},{8,9},{9,8},{10,11... | collective-permute-start | bytes 4718600 | tf_op jit(solution)/shard_map/ppermute | solution.py:223
  427.5 19.5 %copy-start = (bf16[8192,128]{1,0:T(8,128)(2,1)}, bf16[8192,128]{1,0:T(8,128)(2,1)S(1)}, u32[]{:S(2)}) copy-start(bf16[8192,128]{1,0:T(8,128)(2,1)S(1)} %fusion.9.local_ref) | copy-start | bytes 6291460
  442.6 30.5 %all-to-all-start.1 = ((bf16[32,128,128]{2,1,0:T(8,128)(2,1)}), bf16[32,128,128]{2,1,0:T(8,128)(2,1)S(1)}, u32[]{:S(2)}, u32[]{:S(2)}) async-start(bf16[32,128,128]{2,1,0:T(8,128)(2,1)} %bitcast.11), calls=%async_computation.1 | async-start | bytes 2097152 | tf_op jit(solution)/shard_map/all_to_all | solution.py:198
  447.1 28.7 %collective-permute-start.4 = (bf16[8192,128]{1,0:T(8,128)(2,1)S(1)}, bf16[8192,128]{1,0:T(8,128)(2,1)}, u32[]{:S(2)}, u32[]{:S(2)}) collective-permute-start(bf16[8192,128]{1,0:T(8,128)(2,1)S(1)} %fusion.9.local_ref), channel_id=1, source_target_pairs={{0,1},{1,0},{2,3},{3,2},{4,5},{5,4},{6,7},{7,6},{8,9},{9,8},{10,11... | collective-permute-start | bytes 6291464 | tf_op jit(solution)/shard_map/ppermute | solution.py:223
  473.1 24.3 %copy-start.3 = (bf16[32,128,128]{2,1,0:T(8,128)(2,1)}, bf16[32,128,128]{2,1,0:T(8,128)(2,1)S(1)}, u32[]{:S(2)}) copy-start(bf16[32,128,128]{2,1,0:T(8,128)(2,1)S(1)} %all-to-all-done.1) | copy-start | bytes 3145732
  473.1 2.7 collective-permute-start.5
  475.8 1.0 copy-start.7
  497.4 331.1 %collective-permute-start.6 = (f32[3072,128]{1,0:T(8,128)}, f32[3072,128]{1,0:T(8,128)S(1)}, u32[]{:S(2)}, u32[]{:S(2)}) collective-permute-start(f32[3072,128]{1,0:T(8,128)} %get-tuple-element.18), channel_id=1, source_target_pairs={{0,1},{1,0},{2,3},{3,2},{4,5},{5,4},{6,7},{7,6},{8,9},{9,8},{10,11... | collective-permute-start | bytes 4718600 | tf_op jit(solution)/shard_map/ppermute | solution.py:223
